TPU v7x, 128 devices: a whole 4x4x4 slice. The times are simulated.
128 devices in a mesh: gen: 4 (over y), dec: 32 (over x, z, core).
Axes of the slice: x: 4, y: 4, z: 4, core: 2. Of those that a mesh axis runs over, the one named last changes fastest.
Arguments:
- latent: bfloat16 [3072, 4, 256], P(('gen', 'dec')), may hold values from -6 to 6
- latent_owner: int32 [3072, 1], P(('gen', 'dec')), may hold values from 0 to 3; in each aligned block of 24 rows (0 to 23, 24 to 47, ...) at most 8 rows name the same one
- next_owner: int32 [4096], P(('gen', 'dec')), may hold values from 0 to 31, as said below
- cache_latent: bfloat16 [4096, 2, 256], P(('gen', 'dec')), may hold values from -6 to 6
- cache_act: bfloat16 [4096, 2, 8192], P(('gen', 'dec')), may hold values from -6 to 6
- weight_in: bfloat16 [3, 144, 512], replicated, may hold values from -0.3125 to 0.3125
- bias_in: float32 [512], replicated, may hold values from -3 to 3
- norm_gain: float32 [512], replicated, may hold values from 0.1 to 1.9
- norm_shift: float32 [512], replicated, may hold values from -3 to 3
- weight_mid: bfloat16 [3, 4608, 512], replicated, may hold values from -0.0546875 to 0.0546875
- bias_mid: float32 [512], replicated, may hold values from -3 to 3
Outputs:
- features: bfloat16 [4096, 4, 8192], P(('gen', 'dec'))
- conv_out: bfloat16 [4096, 4, 8192], P(('gen', 'dec'))
- next_latent: bfloat16 [4096, 2, 256], P(('gen', 'dec'))
- next_act: bfloat16 [4096, 2, 8192], P(('gen', 'dec'))
Inputs may be any that keep to these rules, and one draw needn't show every extreme that they name: `latent_owner`: among one device's 24 clips at most 8 name the same index of gen, and in some devices exactly 8 do. `next_owner`: one device's 32 decode slots name one index of dec at most 2 times, and every device's slots name some index exactly 2 times; among the devices of one index of gen, every index of dec is named by exactly 32 slots. Slots with live_mask 0 are named too.
All inputs are finite; a program needn't handle non-finite values.
Results may differ from a plain program's by a relative error of at most 0.0051.
Values may be sent and summed in bfloat16 or wider, within the bound.
A program may use at most 320 MiB of HBM per device.

v0:
```python
import functools

import jax
import jax.numpy as jnp
import numpy as np
from jax import lax
from jax.experimental import pallas as pl
from jax.experimental.pallas import tpu as pltpu
from jax.sharding import PartitionSpec as P

BF = jnp.bfloat16
F32 = jnp.float32
I32 = jnp.int32

N_GEN, N_DEC = 4, 32
GEN, CAP_L, DSLOTS, CAP_C = 24, 8, 32, 2
FR, CELLS, HT, WT, LAT, CH = 4, 16, 4, 4, 16, 512
MSG_A = 48
MSG_B = 16
EPSILON = 1e-06

TAPS = [4, 1, 3, 5, 7, 0, 2, 6, 8]
REST_CELLS = [y * WT + x for y in range(3) for x in range(3)]
PLAIN_CELLS = [c for c in range(CELLS) if c not in REST_CELLS]


def tap_cells(tap):
    dy, dx = tap // 3 - 1, tap % 3 - 1
    pairs = []
    for y in range(HT):
        for x in range(WT):
            if 0 <= y + dy < HT and 0 <= x + dx < WT:
                pairs.append((y * WT + x, (y + dy) * WT + x + dx))
    return pairs


def patch_selectors():
    first = np.zeros((LAT * CELLS, CELLS * 128), np.float32)
    for tap in range(8):
        for cell, source in tap_cells(tap):
            for e in range(LAT):
                first[e * CELLS + source, cell * 128 + tap * LAT + e] = 1
    rest = np.zeros((3 * LAT * CELLS, len(REST_CELLS) * 128), np.float32)
    for cell, source in tap_cells(8):
        at = REST_CELLS.index(cell)
        for a in range(3):
            for e in range(LAT):
                rest[a * 256 + e * CELLS + source, at * 128 + a * LAT + e] = 1
    return jnp.asarray(first, BF), jnp.asarray(rest, BF)


def dot(a, b):
    return jnp.dot(a, b, preferred_element_type=F32)


def iota(shape, dim):
    return lax.broadcasted_iota(I32, shape, dim)


def onehot(mask):
    return jnp.where(mask, 1.0, 0.0).astype(BF)


def ranked_codes(row, length, per, places):
    sub = iota((length, length), 0)
    lane = iota((length, length), 1)
    wide = jnp.broadcast_to(row, (length, length))
    col = jnp.sum(jnp.where(sub == lane, wide, 0.0), axis=1, keepdims=True)
    same = (wide == col) & (lane < sub)
    rank = jnp.sum(jnp.where(same, 1.0, 0.0), axis=1, keepdims=True)
    return col * per + rank


def spread(codes, where_to, length, width):
    hit = iota((length, width), 0) == where_to
    found = jnp.sum(jnp.where(hit, codes + 1.0, 0.0), axis=0, keepdims=True)
    return found - 1.0


def exchange_kernel(
    latent_ref, owner_ref, next_ref, clips_out, next_out,
    send_a, recv_a, send_b, recv_b, sem_sa, sem_ra, sem_sb, sem_rb,
):
    g = lax.axis_index("gen")
    d = lax.axis_index("dec")
    barrier = pltpu.get_barrier_semaphore()

    def greet_gen(i, _):
        pl.semaphore_signal(barrier, inc=1, device_id={"gen": lax.rem(g + i, N_GEN)},
                            device_id_type=pl.DeviceIdType.MESH)
        return 0

    def greet_dec(i, _):
        pl.semaphore_signal(barrier, inc=1, device_id={"dec": lax.rem(d + i, N_DEC)},
                            device_id_type=pl.DeviceIdType.MESH)
        return 0

    lax.fori_loop(1, N_GEN, greet_gen, 0)
    lax.fori_loop(1, N_DEC, greet_dec, 0)

    codes = ranked_codes(owner_ref[...].astype(F32), GEN, CAP_L, N_GEN)
    lane = iota((GEN, 128), 1)
    clip_at = jnp.where(lane < 96, lane // 4, jnp.where(lane < 96 + GEN, lane - 96, -1))
    lanes = spread(codes, clip_at, GEN, 128)
    row = iota((N_GEN * MSG_A, 128), 0)
    col = iota((N_GEN * MSG_A, 128), 1)
    part = row % MSG_A
    kind = part // 8
    want = ((row // MSG_A) * CAP_L + part % 8).astype(F32)
    col_kind = jnp.where(col < 96, col % 4, 4)
    pick = (want == lanes) & (kind == col_kind)
    pick = pick | ((kind == 5) & (col == 127))
    rows = latent_ref[...].reshape(GEN * FR, LAT * CELLS)
    rows = jnp.concatenate([rows, jnp.ones((32, LAT * CELLS), BF)], axis=0)
    send_a[...] = dot(onehot(pick), rows).astype(BF).reshape(send_a.shape)
    recv_a[g] = send_a[g]

    pl.semaphore_wait(barrier, N_GEN - 1 + N_DEC - 1)

    def copy_a(target, landed):
        return pltpu.make_async_remote_copy(
            src_ref=send_a.at[target], dst_ref=recv_a.at[landed],
            send_sem=sem_sa.at[target], recv_sem=sem_ra.at[landed],
            device_id={"gen": target}, device_id_type=pl.DeviceIdType.MESH,
        )

    for i in range(1, N_GEN):
        copy_a(lax.rem(g + i, N_GEN), g).start()

    codes_b = ranked_codes(next_ref[...].astype(F32), DSLOTS, CAP_C, N_DEC)
    lane_b = iota((DSLOTS, N_GEN * MSG_A), 1)
    slot_at = (lane_b // MSG_A) * CAP_L + lane_b % 8
    lanes_b = spread(codes_b, slot_at, DSLOTS, N_GEN * MSG_A)
    row_b = iota((N_DEC * MSG_B, N_GEN * MSG_A), 0)
    col_b = iota((N_DEC * MSG_B, N_GEN * MSG_A), 1)
    want_b = ((row_b // MSG_B) * CAP_C + row_b % 2).astype(F32)
    pick_b = onehot((want_b == lanes_b) & ((row_b % MSG_B) // 2 == (col_b % MSG_A) // 8))

    for i in range(1, N_GEN):
        other = lax.rem(g + i, N_GEN)
        copy_a(other, other).wait_recv()

    got = recv_a[...].reshape(N_GEN * MSG_A, LAT * CELLS)
    send_b[...] = dot(pick_b, got).astype(BF).reshape(send_b.shape)

    def copy_b(target, landed):
        return pltpu.make_async_remote_copy(
            src_ref=send_b.at[target], dst_ref=recv_b.at[landed],
            send_sem=sem_sb.at[target], recv_sem=sem_rb.at[landed],
            device_id={"dec": target}, device_id_type=pl.DeviceIdType.MESH,
        )

    def start_b(i, _):
        copy_b(lax.rem(d + i, N_DEC), d).start()
        return 0

    lax.fori_loop(1, N_DEC, start_b, 0)
    recv_b[d] = send_b[d]
    clips_out[...] = got

    def take_b(i, _):
        other = lax.rem(d + i, N_DEC)
        copy_b(other, other).wait_recv()
        return 0

    lax.fori_loop(1, N_DEC, take_b, 0)
    next_out[...] = recv_b[...].reshape(N_DEC * MSG_B, LAT * CELLS)

    for i in range(1, N_GEN):
        copy_a(lax.rem(g + i, N_GEN), g).wait_send()

    def sent_b(i, _):
        copy_b(lax.rem(d + i, N_DEC), d).wait_send()
        return 0

    lax.fori_loop(1, N_DEC, sent_b, 0)


def exchange(latent, owner_row, next_row):
    vmem = pl.BlockSpec(memory_space=pltpu.VMEM)
    return pl.pallas_call(
        exchange_kernel,
        out_shape=(
            jax.ShapeDtypeStruct((N_GEN * MSG_A, LAT * CELLS), BF),
            jax.ShapeDtypeStruct((N_DEC * MSG_B, LAT * CELLS), BF),
        ),
        in_specs=[vmem] * 3,
        out_specs=(vmem, vmem),
        scratch_shapes=[
            pltpu.VMEM((N_GEN, MSG_A, LAT * CELLS), BF),
            pltpu.VMEM((N_GEN, MSG_A, LAT * CELLS), BF),
            pltpu.VMEM((N_DEC, MSG_B, LAT * CELLS), BF),
            pltpu.VMEM((N_DEC, MSG_B, LAT * CELLS), BF),
            pltpu.SemaphoreType.DMA((N_GEN,)),
            pltpu.SemaphoreType.DMA((N_GEN,)),
            pltpu.SemaphoreType.DMA((N_DEC,)),
            pltpu.SemaphoreType.DMA((N_DEC,)),
        ],
        compiler_params=pltpu.CompilerParams(
            collective_id=0, has_side_effects=True, vmem_limit_bytes=16 << 20
        ),
        name="exchange",
    )(latent, owner_row, next_row)


def group_mean(total, spread_groups):
    high = total.astype(BF)
    left = total - high.astype(F32)
    mid = left.astype(BF)
    low = (left - mid.astype(F32)).astype(BF)
    return dot(high, spread_groups) + dot(mid, spread_groups) + dot(low, spread_groups)


def silu(u):
    half = 0.5 * u
    return half + half * jnp.tanh(half)


def decode_kernel(
    clips_ref, next_ref, cache_lat_ref, w_in_ref, bias_in_ref, gain_ref, shift_ref,
    bias_mid_ref, sel_ref, rest_ref, hist_hbm, w_mid_hbm,
    feat_hbm, conv_hbm, nlat_ref, nact_hbm,
    hist, w_mid, feat, act, trans, sums, mixed, feat_out, nact_out,
    sem_in, sem_w, sem_out,
):
    hist_copy = pltpu.make_async_copy(hist_hbm, hist, sem_in)
    hist_copy.start()
    w_copies = []
    for at, tap in enumerate(TAPS):
        copy = pltpu.make_async_copy(
            w_mid_hbm.at[:, pl.ds(tap * CH, CH), :], w_mid.at[at], sem_w.at[at]
        )
        copy.start()
        w_copies.append(copy)

    bias_in = bias_in_ref[...].reshape(1, CH)
    gain = gain_ref[...].reshape(1, CH)
    shift = shift_ref[...].reshape(1, CH)
    bias_mid = bias_mid_ref[...].reshape(1, CH)
    groups = (iota((CH, CH), 0) // 16) == (iota((CH, CH), 1) // 16)
    groups = jnp.where(groups, 1.0 / 256.0, 0.0).astype(BF)
    w_cat = jnp.concatenate(
        [w_in_ref[a, :128, :] for a in range(3)]
        + [w_in_ref[a, 128:144, :] for a in range(3)]
        + [jnp.zeros((80, CH), BF)],
        axis=0,
    )

    def normalised(read, write, rows):
        total = jnp.zeros((rows, CH), F32)
        for c in range(CELLS):
            total = total + read(c).astype(F32)
        center = group_mean(total, groups)
        square = jnp.zeros((rows, CH), F32)
        for c in range(CELLS):
            off = read(c).astype(F32) - center
            square = square + off * off
        scale = lax.rsqrt(group_mean(square, groups) + EPSILON) * gain
        for c in range(CELLS):
            u = (read(c).astype(F32) - center) * scale + shift
            write(c, silu(u).astype(BF))

    def features_of(frames, rows, write, live):
        shifted = [frames[a * 32:a * 32 + rows] for a in range(3)]
        taps = dot(frames, sel_ref[...]).astype(BF)
        rest = dot(jnp.concatenate(shifted, axis=1), rest_ref[...]).astype(BF)
        for cells, depth in ((REST_CELLS, 512), (PLAIN_CELLS, 384)):
            left = []
            for c in cells:
                block = [taps[a * 32:a * 32 + rows, c * 128:c * 128 + 128] for a in range(3)]
                if depth == 512:
                    at = REST_CELLS.index(c)
                    block.append(rest[:, at * 128:at * 128 + 128])
                left.append(jnp.concatenate(block, axis=1))
            made = dot(jnp.concatenate(left, axis=0), w_cat[:depth])
            for i, c in enumerate(cells):
                write(c, ((made[i * rows:(i + 1) * rows] + bias_in) * live).astype(BF))

    row = iota((320, 256), 0)
    col = iota((320, 256), 1)
    frame, slot = row // 32, row % 32
    clip_row = (slot // 8) * MSG_A + jnp.where(row < 192, frame - 2, 4) * 8 + slot % 8
    source_row = jnp.where(row < 64, 192 + slot * 2 + frame, clip_row)
    stacked = jnp.concatenate([clips_ref[...], cache_lat_ref[...].reshape(64, 256)], axis=0)
    placed = dot(onehot(col == source_row), stacked)
    frames = placed[:192].astype(BF)
    live = jnp.concatenate([placed[192:], placed[192:]], axis=1)

    def put_feat(c, value):
        feat[c] = value

    features_of(frames, 128, put_feat, live)

    def put_act(c, value):
        act[c] = value

    normalised(lambda c: feat[c], put_act, 128)

    hist_copy.wait()
    turn = onehot(iota((64, 64), 1) == (iota((64, 64), 0) % 32) * 2 + iota((64, 64), 0) // 32)
    for c in range(CELLS):
        old = dot(turn, hist[:, :, c * CH:(c + 1) * CH].reshape(64, CH)).astype(BF)
        q = [old[:32], old[32:]] + [act[c, t * 32:t * 32 + 32] for t in range(4)]
        for tile in range(2):
            d0, d1, d2, d3 = q[2 * tile:2 * tile + 4]
            at = slice(tile * 32, tile * 32 + 32)
            trans[0, c, at] = d0 - d2
            trans[1, c, at] = d1 + d2
            trans[2, c, at] = d2 - d1
            trans[3, c, at] = d1 - d3

    order = onehot(
        iota((128, 128), 1) == (iota((128, 128), 0) % 4) * 32 + iota((128, 128), 0) // 4
    )
    for c in range(CELLS):
        turned = dot(order, feat[c]).astype(BF).reshape(32, 4, CH)
        feat_out[:, :, c * CH:(c + 1) * CH] = turned
    feat_copy = pltpu.make_async_copy(feat_out, feat_hbm, sem_out.at[0])
    feat_copy.start()

    flags = lax.dot_general(
        onehot(iota((8, 256), 1) == 0), next_ref[...], (((1,), (1,)), ((), ())),
        preferred_element_type=F32,
    ).astype(BF)
    big = iota((512, 128), 0)
    index = (big // MSG_B) * 2 + big % 2
    filled = dot(flags, onehot(((big % MSG_B) // 2 == 5) & (index == iota((512, 128), 1))))
    before = onehot(iota((128, 128), 0) < iota((128, 128), 1))
    place = dot(filled.astype(BF), before)
    take = (filled[:1] > 0.5) & (place[:1] == iota((32, 128), 0).astype(F32))
    take = onehot(take)
    lane = iota((128, 512), 1)
    lane_index = (lane // MSG_B) * 2 + lane % 2
    entry = lane_index == iota((128, 512), 0)
    picks = [
        dot(take, onehot(entry & ((lane % MSG_B) // 2 == kind))).astype(BF) for kind in range(5)
    ]
    moved = dot(jnp.concatenate(picks, axis=0), next_ref[...])
    later = moved[:128].astype(BF)
    live_next = jnp.concatenate([moved[128:160], moved[128:160]], axis=1)
    live_next = jnp.concatenate([live_next, live_next], axis=0)
    pair = onehot(iota((64, 64), 1) == (iota((64, 64), 0) % 2) * 32 + iota((64, 64), 0) // 2)
    nlat_ref[...] = dot(pair, later[64:]).astype(BF).reshape(32, 2, 256)

    features_of(later, 64, lambda c, value: mixed.__setitem__(c, value), live_next)

    def put_next(c, value):
        value = (value.astype(F32) * live_next).astype(BF)
        nact_out[:, :, c * CH:(c + 1) * CH] = dot(pair, value).astype(BF).reshape(32, 2, CH)

    normalised(lambda c: mixed[c], put_next, 64)
    nact_copy = pltpu.make_async_copy(nact_out, nact_hbm, sem_out.at[1])
    nact_copy.start()

    for at, tap in enumerate(TAPS):
        w_copies[at].wait()
        g0 = w_mid[at, 0].astype(F32)
        g1 = w_mid[at, 1].astype(F32)
        g2 = w_mid[at, 2].astype(F32)
        ends = g0 + g2
        weights = [
            w_mid[at, 0], ((ends + g1) * 0.5).astype(BF), ((ends - g1) * 0.5).astype(BF),
            w_mid[at, 2],
        ]
        pairs = tap_cells(tap)
        for j in range(4):
            left = jnp.concatenate([trans[j, source] for _, source in pairs], axis=0)
            made = dot(left, weights[j])
            for i, (cell, _) in enumerate(pairs):
                piece = made[i * 64:(i + 1) * 64]
                if at == 0:
                    sums[j, cell] = piece
                else:
                    sums[j, cell] += piece

    r128 = iota((128, 128), 0)
    back = onehot(iota((128, 128), 1) == (r128 % 2) * 64 + ((r128 % 4) // 2) * 32 + r128 // 4)
    keep = live[:64]
    feat_copy.wait()
    conv_out = feat_out
    conv_copies = []
    for c in range(CELLS):
        both = sums[1, c] + sums[2, c]
        apart = sums[1, c] - sums[2, c]
        even = ((sums[0, c] + both + bias_mid) * keep).astype(BF)
        odd = ((apart - sums[3, c] + bias_mid) * keep).astype(BF)
        turned = dot(back, jnp.concatenate([even, odd], axis=0)).astype(BF)
        conv_out[:, :, c * CH:(c + 1) * CH] = turned.reshape(32, 4, CH)
        if c % 4 == 3:
            lanes = pl.ds((c - 3) * CH, 4 * CH)
            copy = pltpu.make_async_copy(
                conv_out.at[:, :, lanes], conv_hbm.at[:, :, lanes], sem_out.at[2 + c // 4]
            )
            copy.start()
            conv_copies.append(copy)
    for copy in [nact_copy] + conv_copies:
        copy.wait()


def decode(clips, later, cache_latent, cache_act, weight_in, bias_in, gain, shift,
           weight_mid, bias_mid):
    sel, rest = patch_selectors()
    vmem = pl.BlockSpec(memory_space=pltpu.VMEM)
    hbm = pl.BlockSpec(memory_space=pl.ANY)
    wide = CELLS * CH
    return pl.pallas_call(
        decode_kernel,
        out_shape=(
            jax.ShapeDtypeStruct((DSLOTS, FR, wide), BF),
            jax.ShapeDtypeStruct((DSLOTS, FR, wide), BF),
            jax.ShapeDtypeStruct((DSLOTS, 2, LAT * CELLS), BF),
            jax.ShapeDtypeStruct((DSLOTS, 2, wide), BF),
        ),
        in_specs=[vmem] * 10 + [hbm, hbm],
        out_specs=(hbm, hbm, vmem, hbm),
        scratch_shapes=[
            pltpu.VMEM((DSLOTS, 2, wide), BF),
            pltpu.VMEM((9, 3, CH, CH), BF),
            pltpu.VMEM((CELLS, 128, CH), BF),
            pltpu.VMEM((CELLS, 128, CH), BF),
            pltpu.VMEM((4, CELLS, 64, CH), BF),
            pltpu.VMEM((4, CELLS, 64, CH), F32),
            pltpu.VMEM((CELLS, 64, CH), BF),
            pltpu.VMEM((DSLOTS, FR, wide), BF),
            pltpu.VMEM((DSLOTS, 2, wide), BF),
            pltpu.SemaphoreType.DMA,
            pltpu.SemaphoreType.DMA((9,)),
            pltpu.SemaphoreType.DMA((6,)),
        ],
        compiler_params=pltpu.CompilerParams(vmem_limit_bytes=58 << 20),
        name="decode",
    )(clips, later, cache_latent, weight_in, bias_in, gain, shift, bias_mid, sel, rest,
      cache_act, weight_mid)


def shards(latent, latent_owner, next_owner, cache_latent, cache_act, weight_in, bias_in,
           norm_gain, norm_shift, weight_mid, bias_mid):
    clips, later = exchange(
        latent, latent_owner.reshape(1, GEN), next_owner.reshape(1, DSLOTS)
    )
    return decode(clips, later, cache_latent, cache_act, weight_in, bias_in, norm_gain,
                  norm_shift, weight_mid, bias_mid)


def solution(mesh):
    both = ("gen", "dec")
    in_specs = (
        P(both, None, None), P(both, None), P(both), P(both, None, None), P(both, None, None),
        P(), P(), P(), P(), P(), P(),
    )
    out_specs = (P(both, None, None),) * 4
    return jax.shard_map(shards, mesh=mesh, in_specs=in_specs, out_specs=out_specs, check_vma=False)
```

profile of v0, /device:TPU:1, one launch (start us, length us, event | category | flops | bytes accessed | tf_op | source)
XLA Modules:
  0.0 53.8 jit_solution(15808529354593615053)
XLA Ops:
  0.6 0.0 copy-start.2
  0.6 0.8 %copy-done.2 = bf16[24,4,256]{2,1,0:T(4,128)(2,1)S(1)} copy-done((bf16[24,4,256]{2,1,0:T(4,128)(2,1)S(1)}, bf16[24,4,256]{2,1,0:T(4,128)(2,1)}, u32[]{:S(2)}) %copy-start.2) | copy-done | bytes 49176
  1.4 0.0 copy-start.3
  1.4 0.7 %copy-done.3 = s32[24,1]{0,1:T(1,128)S(1)} copy-done((s32[24,1]{0,1:T(1,128)S(1)}, s32[24,1]{0,1:T(1,128)}, u32[]{:S(2)}) %copy-start.3) | copy-done | bytes 120
  2.1 0.0 copy-start.4
  2.1 0.7 %copy-done.4 = s32[32]{0:T(128)S(1)} copy-done((s32[32]{0:T(128)S(1)}, s32[32]{0:T(128)}, u32[]{:S(2)}) %copy-start.4) | copy-done | bytes 152
  2.7 18.7 %exchange.1 = (bf16[192,256]{1,0:T(8,128)(2,1)S(1)}, bf16[512,256]{1,0:T(8,128)(2,1)S(1)}) custom-call(bf16[24,4,256]{2,1,0:T(4,128)(2,1)S(1)} %copy-done.2, s32[1,24]{1,0:T(1,128)S(1)} %bitcast.2, s32[1,32]{1,0:T(1,128)S(1)} %bitcast.3), custom_call_target="tpu_custom_call" | custom-call | tf_op jit(solution)/shard_map/exchange/pallas_call | solution.py:181
  21.5 0.0 copy-start
  21.5 0.7 %copy-done = bf16[512,256]{1,0:T(8,128)(2,1)} copy-done((bf16[512,256]{1,0:T(8,128)(2,1)}, bf16[512,256]{1,0:T(8,128)(2,1)S(1)}, u32[]{:S(2)}) %copy-start) | copy-done | bytes 262168
  22.2 0.0 copy-start.1
  22.2 0.6 %copy-done.1 = bf16[192,256]{1,0:T(8,128)(2,1)} copy-done((bf16[192,256]{1,0:T(8,128)(2,1)}, bf16[192,256]{1,0:T(8,128)(2,1)S(1)}, u32[]{:S(2)}) %copy-start.1) | copy-done | bytes 98328
  22.8 30.9 %decode.1 = (bf16[32,4,8192]{2,1,0:T(4,128)(2,1)}, bf16[32,4,8192]{2,1,0:T(4,128)(2,1)}, bf16[32,2,256]{2,1,0:T(2,128)(2,1)}, bf16[32,2,8192]{2,1,0:T(2,128)(2,1)}) custom-call(bf16[192,256]{1,0:T(8,128)(2,1)} %copy-done.1, bf16[512,256]{1,0:T(8,128)(2,1)} %copy-done, bf16[32,2,256]{2,1,0:T(2,128)(2,1)} %cache_lat_ref.1, bf16[3,144,512]{2,1,0:T(8,128)(2,1)} %w_in_ref.1, ...), custom_call_target="tpu_custom_call" | custom-call | tf_op jit(solution)/shard_map/decode/pallas_call | solution.py:406
Async XLA Ops:
  0.6 0.8 %copy-start.2 = (bf16[24,4,256]{2,1,0:T(4,128)(2,1)S(1)}, bf16[24,4,256]{2,1,0:T(4,128)(2,1)}, u32[]{:S(2)}) copy-start(bf16[24,4,256]{2,1,0:T(4,128)(2,1)} %latent_ref.1) | copy-start | bytes 147460
  1.4 0.7 %copy-start.3 = (s32[24,1]{0,1:T(1,128)S(1)}, s32[24,1]{0,1:T(1,128)}, u32[]{:S(2)}) copy-start(s32[24,1]{0,1:T(1,128)} %param.14) | copy-start | bytes 292
  2.1 0.7 %copy-start.4 = (s32[32]{0:T(128)S(1)}, s32[32]{0:T(128)}, u32[]{:S(2)}) copy-start(s32[32]{0:T(128)} %param.15) | copy-start | bytes 388
  21.5 0.7 %copy-start = (bf16[512,256]{1,0:T(8,128)(2,1)}, bf16[512,256]{1,0:T(8,128)(2,1)S(1)}, u32[]{:S(2)}) copy-start(bf16[512,256]{1,0:T(8,128)(2,1)S(1)} %get-tuple-element.7.next_ref) | copy-start | bytes 786436
  22.2 0.6 %copy-start.1 = (bf16[192,256]{1,0:T(8,128)(2,1)}, bf16[192,256]{1,0:T(8,128)(2,1)S(1)}, u32[]{:S(2)}) copy-start(bf16[192,256]{1,0:T(8,128)(2,1)S(1)} %get-tuple-element.6.clips_ref) | copy-start | bytes 294916
where the time goes:
time: 54 us; the launch traced here: 53.8 us
  Pallas kernels  49.6 us (92%)
  local copies, waits for them, and re-layouts  3.43 us (6%)
  between operations  0.82 us (2%)
    pallas_call x1, Pallas kernels, decode(): pl.pallas_call(decode_kernel, out_shape=(jax.ShapeDtypeStruct((DSLOTS, FR...  30.9 us
    pallas_call x1, Pallas kernels, exchange(): pl.pallas_call(exchange_kernel, out_shape=(jax.ShapeDtypeStruct((N_GEN *...  18.7 us
    unnamed x10, local copies, waits for them, and re-layouts  3.43 us

commit v1 on v0

v1 whole, which is shorter than its diff:
```python
import functools

import jax
import jax.numpy as jnp
import numpy as np
from jax import lax
from jax.experimental import pallas as pl
from jax.experimental.pallas import tpu as pltpu
from jax.sharding import PartitionSpec as P

BF = jnp.bfloat16
F32 = jnp.float32
I32 = jnp.int32

N_GEN, N_DEC = 4, 32
GEN, CAP_L, DSLOTS, CAP_C = 24, 8, 32, 2
FR, CELLS, HT, WT, LAT, CH = 4, 16, 4, 4, 16, 512
PART = 8
MSG_A = CAP_L * PART
MSG_B = CAP_C * PART
DEAD, EMPTY = 64.0, 128.0
EPSILON = 1e-06

AHEAD = 3
LIM = 65400 << 10
TAPS = [4, 1, 3, 5, 7, 0, 2, 6, 8]
REST_CELLS = [y * WT + x for y in range(3) for x in range(3)]
PLAIN_CELLS = [c for c in range(CELLS) if c not in REST_CELLS]


def tap_cells(tap):
    dy, dx = tap // 3 - 1, tap % 3 - 1
    pairs = []
    for y in range(HT):
        for x in range(WT):
            if 0 <= y + dy < HT and 0 <= x + dx < WT:
                pairs.append((y * WT + x, (y + dy) * WT + x + dx))
    return pairs


def patch_selectors():
    first = np.zeros((LAT * CELLS, CELLS * 128), np.float32)
    for tap in range(8):
        for cell, source in tap_cells(tap):
            for e in range(LAT):
                first[e * CELLS + source, cell * 128 + tap * LAT + e] = 1
    rest = np.zeros((3 * LAT * CELLS, len(REST_CELLS) * 128), np.float32)
    for cell, source in tap_cells(8):
        at = REST_CELLS.index(cell)
        for a in range(3):
            for e in range(LAT):
                rest[a * 256 + e * CELLS + source, at * 128 + a * LAT + e] = 1
    return jnp.asarray(first, BF), jnp.asarray(rest, BF)


def dot(a, b):
    return jnp.dot(a, b, preferred_element_type=F32)


def iota(shape, dim):
    return lax.broadcasted_iota(I32, shape, dim)


def onehot(mask):
    return jnp.where(mask, 1.0, 0.0).astype(BF)


def ranked_codes(row, length, per):
    sub = iota((length, length), 0)
    lane = iota((length, length), 1)
    wide = jnp.broadcast_to(row, (length, length))
    col = jnp.sum(jnp.where(sub == lane, wide, 0.0), axis=1, keepdims=True)
    same = (wide == col) & (lane < sub)
    rank = jnp.sum(jnp.where(same, 1.0, 0.0), axis=1, keepdims=True)
    return col * per + rank


def spread(codes, where_to, length, width):
    hit = iota((length, width), 0) == where_to
    found = jnp.sum(jnp.where(hit, codes + 1.0, 0.0), axis=0, keepdims=True)
    return found - 1.0


def group_mean(total, spread_groups):
    high = total.astype(BF)
    left = total - high.astype(F32)
    mid = left.astype(BF)
    low = (left - mid.astype(F32)).astype(BF)
    return dot(high, spread_groups) + dot(mid, spread_groups) + dot(low, spread_groups)


def silu(u):
    half = 0.5 * u
    return half + half * jnp.tanh(half)


def block_ones():
    same = (iota((CH, CH), 0) // 16) == (iota((CH, CH), 1) // 16)
    return jnp.where(same, 1.0 / 256.0, 0.0).astype(BF)


def input_weights(w_in_ref):
    return jnp.concatenate(
        [w_in_ref[a, :128, :] for a in range(3)]
        + [w_in_ref[a, 128:144, :] for a in range(3)]
        + [jnp.zeros((80, CH), BF)],
        axis=0,
    )


def normalised(read, write, rows, groups, gain, shift):
    total = jnp.zeros((rows, CH), F32)
    for c in range(CELLS):
        total = total + read(c).astype(F32)
    center = group_mean(total, groups)
    square = jnp.zeros((rows, CH), F32)
    for c in range(CELLS):
        off = read(c).astype(F32) - center
        square = square + off * off
    scale = lax.rsqrt(group_mean(square, groups) + EPSILON) * gain
    for c in range(CELLS):
        u = (read(c).astype(F32) - center) * scale + shift
        write(c, silu(u).astype(BF))


def patches(frames, rows, sel, rest):
    shifted = [frames[a * 32:a * 32 + rows] for a in range(3)]
    return (
        dot(frames, sel[...]).astype(BF),
        dot(jnp.concatenate(shifted, axis=1), rest[...]).astype(BF),
    )


def features_of(found, rows, w_cat, bias, live, write, groups):
    taps, rest = found
    for cells in groups:
        depth = 512 if cells[0] in REST_CELLS else 384
        left = []
        for c in cells:
            block = [taps[a * 32:a * 32 + rows, c * 128:c * 128 + 128] for a in range(3)]
            if depth == 512:
                at = REST_CELLS.index(c)
                block.append(rest[:, at * 128:at * 128 + 128])
            left.append(jnp.concatenate(block, axis=1))
        made = dot(jnp.concatenate(left, axis=0), w_cat[:depth])
        for i, c in enumerate(cells):
            write(c, ((made[i * rows:(i + 1) * rows] + bias) * live).astype(BF))


def lane_halves(pick_row, pick_col_of, source):
    return jnp.concatenate(
        [dot(onehot(pick_row == pick_col_of(half)), source) for half in range(2)], axis=1
    )


def front_kernel(
    latent_hbm, owner_hbm, next_hbm, cache_hbm, hist_hbm, w_in_hbm, bias_hbm, gain_hbm,
    shift_hbm, sel_hbm, rest_hbm,
    trans_hbm, feat_hbm, live_hbm, later_hbm,
    latent, owner, nexts, cache, hist, w_in, bias_v, gain_v, shift_v, sel, rest,
    send_a, recv_a, send_b, recv_x, recv_z, recv_c, feat, old, trans, live_v,
    sem_in, sem_out, sem_sa, sem_ra, sem_sx, sem_rx, sem_sz, sem_rz, sem_sc, sem_rc,
):
    g = lax.axis_index("gen")
    d = lax.axis_index("dec")
    x, z, c = d // 8, (d // 2) % 4, d % 2
    gens = [lax.rem(g + i, 4) for i in (1, 2, 3)]
    xs = [lax.rem(x + i, 4) for i in (1, 2, 3)]
    zs = [lax.rem(z + i, 4) for i in (1, 2, 3)]
    mesh_ids = pl.DeviceIdType.MESH
    barrier = pltpu.get_barrier_semaphore()
    peers = [{"gen": p} for p in gens]
    peers += [{"dec": p * 8 + z * 2 + c} for p in xs]
    peers += [{"dec": x * 8 + p * 2 + c} for p in zs]
    peers += [{"dec": x * 8 + z * 2 + (1 - c)}]
    for peer in peers:
        pl.semaphore_signal(barrier, inc=1, device_id=peer, device_id_type=mesh_ids)

    loads = []
    for i, (src, dst) in enumerate((
        (latent_hbm, latent), (owner_hbm, owner), (next_hbm, nexts), (cache_hbm, cache),
        (hist_hbm, hist), (sel_hbm, sel), (rest_hbm, rest), (w_in_hbm, w_in),
        (bias_hbm, bias_v), (gain_hbm, gain_v), (shift_hbm, shift_v),
    )):
        load = pltpu.make_async_copy(src, dst, sem_in.at[i])
        load.start()
        loads.append(load)

    loads[0].wait()
    loads[1].wait()
    loads[2].wait()
    codes = ranked_codes(owner[...].astype(F32), GEN, CAP_L)
    lane = iota((GEN, 256), 1)
    clip_at = jnp.where(lane < 192, (lane % 96) // 4, -1)
    lanes = spread(codes, clip_at, GEN, 256)
    row = iota((N_GEN * MSG_A, 256), 0)
    col = iota((N_GEN * MSG_A, 256), 1)
    named = ((row // MSG_A) * CAP_L + (row % MSG_A) // PART).astype(F32) == lanes
    pick = named & ((row % PART) == (col % 4) * 2 + col // 96) & (col < 192)
    present = jnp.sum(jnp.where(pick, 1.0, 0.0), axis=1, keepdims=True)
    rows = latent[...].reshape(GEN * FR, LAT * CELLS)
    rows = jnp.concatenate([rows[:, :128], rows[:, 128:], jnp.zeros((64, 128), BF)], axis=0)
    ready = jnp.where(present > 0.5, dot(onehot(pick), rows), DEAD)
    send_a[...] = ready.astype(BF).reshape(send_a.shape)
    recv_a[g] = send_a[g]

    pl.semaphore_wait(barrier, len(peers))

    def copy_a(target, landed):
        return pltpu.make_async_remote_copy(
            src_ref=send_a.at[target], dst_ref=recv_a.at[landed],
            send_sem=sem_sa.at[target], recv_sem=sem_ra.at[landed],
            device_id={"gen": target}, device_id_type=mesh_ids,
        )

    for p in gens:
        copy_a(p, g).start()

    codes_b = ranked_codes(nexts[...].astype(F32), DSLOTS, CAP_C)
    lane_b = iota((DSLOTS, 256), 1)
    lanes_b = spread(codes_b, lane_b // PART, DSLOTS, 256)
    row_b = iota((N_DEC * MSG_B, 256), 0)
    col_b = iota((N_DEC * MSG_B, 256), 1)
    pick_b = ((row_b // PART).astype(F32) == lanes_b) & ((row_b % PART) == (col_b % PART))
    filled = jnp.sum(jnp.where(pick_b, 1.0, 0.0), axis=1, keepdims=True)
    pick_b = onehot(pick_b)
    loads[4].wait()
    turn = onehot(iota((64, 64), 1) == (iota((64, 64), 0) % 32) * 2 + iota((64, 64), 0) // 32)
    for cell in range(CELLS):
        lanes_c = slice(cell * CH, (cell + 1) * CH)
        old[cell] = dot(turn, hist[:, :, lanes_c].reshape(64, CH)).astype(BF)
    loads[3].wait()
    for load in loads[5:]:
        load.wait()
    groups = block_ones()
    w_cat = input_weights(w_in)
    bias = bias_v[...].reshape(1, CH)
    gain = gain_v[...].reshape(1, CH)
    shift = shift_v[...].reshape(1, CH)
    cached = dot(turn, cache[...].reshape(64, 256)).astype(BF)

    for p in gens:
        copy_a(p, p).wait_recv()
    got = recv_a[...].reshape(N_GEN * MSG_A, 128)
    messages = jnp.where(filled > 0.5, dot(pick_b, got), EMPTY)
    send_b[...] = messages.astype(BF).reshape(send_b.shape)

    def copy_x(target, landed):
        return pltpu.make_async_remote_copy(
            src_ref=send_b.at[target], dst_ref=recv_x.at[landed],
            send_sem=sem_sx.at[target], recv_sem=sem_rx.at[landed],
            device_id={"dec": target * 8 + z * 2 + c}, device_id_type=mesh_ids,
        )

    def copy_z(target, landed):
        return pltpu.make_async_remote_copy(
            src_ref=recv_x.at[:, target], dst_ref=recv_z.at[landed],
            send_sem=sem_sz.at[target], recv_sem=sem_rz.at[landed],
            device_id={"dec": x * 8 + target * 2 + c}, device_id_type=mesh_ids,
        )

    def copy_c(target, landed):
        return pltpu.make_async_remote_copy(
            src_ref=recv_z.at[:, :, target], dst_ref=recv_c.at[landed],
            send_sem=sem_sc, recv_sem=sem_rc,
            device_id={"dec": x * 8 + z * 2 + target}, device_id_type=mesh_ids,
        )

    for p in xs:
        copy_x(p, x).start()
    recv_x[x] = send_b[x]

    r128 = iota((128, 256), 0)
    placed = lane_halves(
        iota((128, 256), 1), lambda half: (r128 % 32) * PART + (r128 // 32) * 2 + half, got
    )
    live = jnp.where(placed[:, :1] < 32.0, 1.0, 0.0)
    live_v[...] = jnp.broadcast_to(live[:64], (64, 128))
    fresh = jnp.where(placed > 32.0, 0.0, placed).astype(BF)
    found = patches(jnp.concatenate([cached, fresh], axis=0), 128, sel, rest)

    def put_feat(cell, value):
        feat[cell] = value

    features_of(found, 128, w_cat, bias, live, put_feat, (REST_CELLS,))

    for p in xs:
        copy_x(p, p).wait_recv()
    for p in zs:
        copy_z(p, z).start()
    recv_z[z] = recv_x[:, z]

    features_of(found, 128, w_cat, bias, live, put_feat, (PLAIN_CELLS,))
    outs = [pltpu.make_async_copy(feat, feat_hbm, sem_out.at[0]),
            pltpu.make_async_copy(live_v, live_hbm, sem_out.at[1])]
    for out in outs:
        out.start()

    total = jnp.zeros((128, CH), F32)
    for cell in range(CELLS):
        total = total + feat[cell].astype(F32)
    center = group_mean(total, groups)
    square = jnp.zeros((128, CH), F32)
    for cell in range(CELLS):
        off = feat[cell].astype(F32) - center
        square = square + off * off
    scale = lax.rsqrt(group_mean(square, groups) + EPSILON) * gain

    for p in zs:
        copy_z(p, p).wait_recv()
    copy_c(1 - c, c).start()
    recv_c[c] = recv_z[:, :, c]

    for cell in range(CELLS):
        u = (feat[cell].astype(F32) - center) * scale + shift
        act = silu(u).astype(BF)
        q = [old[cell, :32], old[cell, 32:]] + [act[t * 32:t * 32 + 32] for t in range(4)]
        for tile in range(2):
            d0, d1, d2, d3 = q[2 * tile:2 * tile + 4]
            at = slice(tile * 32, tile * 32 + 32)
            trans[0, cell, at] = d0 - d2
            trans[1, cell, at] = d1 + d2
            trans[2, cell, at] = d2 - d1
            trans[3, cell, at] = d1 - d3
        if cell % 4 == 3:
            part = pl.ds(cell - 3, 4)
            out = pltpu.make_async_copy(
                trans.at[:, part], trans_hbm.at[:, part], sem_out.at[2 + cell // 4]
            )
            out.start()
            outs.append(out)

    copy_c(1 - c, 1 - c).wait_recv()
    out = pltpu.make_async_copy(recv_c, later_hbm, sem_out.at[6])
    out.start()
    outs.append(out)
    for p in gens:
        copy_a(p, g).wait_send()
    for p in xs:
        copy_x(p, x).wait_send()
    for p in zs:
        copy_z(p, z).wait_send()
    copy_c(1 - c, c).wait_send()
    for out in outs:
        out.wait()


def front(latent, owner, nexts, cache_latent, cache_act, weight_in, bias_in, gain, shift, sel, rest):
    hbm = pl.BlockSpec(memory_space=pltpu.HBM)
    wide = CELLS * CH
    dma = pltpu.SemaphoreType.DMA
    return pl.pallas_call(
        front_kernel,
        out_shape=(
            jax.ShapeDtypeStruct((4, CELLS, 64, CH), BF),
            jax.ShapeDtypeStruct((CELLS, 128, CH), BF),
            jax.ShapeDtypeStruct((64, 128), F32),
            jax.ShapeDtypeStruct((2, 4, 4, MSG_B, 128), BF),
        ),
        in_specs=[hbm] * 11,
        out_specs=(hbm,) * 4,
        scratch_shapes=[
            pltpu.VMEM((GEN, FR, LAT * CELLS), BF),
            pltpu.VMEM((1, GEN), I32),
            pltpu.VMEM((1, DSLOTS), I32),
            pltpu.VMEM((DSLOTS, 2, LAT * CELLS), BF),
            pltpu.VMEM((DSLOTS, 2, wide), BF),
            pltpu.VMEM((3, 9 * LAT, CH), BF),
            pltpu.VMEM((CH,), F32),
            pltpu.VMEM((CH,), F32),
            pltpu.VMEM((CH,), F32),
            pltpu.VMEM(sel.shape, BF),
            pltpu.VMEM(rest.shape, BF),
            pltpu.VMEM((N_GEN, MSG_A, 128), BF),
            pltpu.VMEM((N_GEN, MSG_A, 128), BF),
            pltpu.VMEM((4, 4, 2, MSG_B, 128), BF),
            pltpu.VMEM((4, 4, 2, MSG_B, 128), BF),
            pltpu.VMEM((4, 4, 2, MSG_B, 128), BF),
            pltpu.VMEM((2, 4, 4, MSG_B, 128), BF),
            pltpu.VMEM((CELLS, 128, CH), BF),
            pltpu.VMEM((CELLS, 64, CH), BF),
            pltpu.VMEM((4, CELLS, 64, CH), BF),
            pltpu.VMEM((64, 128), F32),
            dma((11,)), dma((7,)), dma((4,)), dma((4,)), dma((4,)), dma((4,)), dma((4,)), dma((4,)),
            dma, dma,
        ],
        compiler_params=pltpu.CompilerParams(
            collective_id=0, has_side_effects=True, vmem_limit_bytes=LIM
        ),
        name="front",
    )(latent, owner, nexts, cache_latent, cache_act, weight_in, bias_in, gain, shift, sel, rest)


def decode_kernel(
    trans_hbm, feat_hbm, live_hbm, later_hbm, w_in_hbm, bias_hbm, gain_hbm, shift_hbm,
    bias_mid_hbm, sel_hbm, rest_hbm, w_mid_hbm,
    feat_out_hbm, conv_hbm, nlat_hbm, nact_hbm,
    trans, feat, live_v, later_v, w_in, bias_v, gain_v, shift_v, bias_mid_v, sel, rest, w_mid,
    sums, mixed, wide_out, nact_out, nlat_out,
    sem_in, sem_w, sem_out,
):
    loads = [
        pltpu.make_async_copy(src, dst, sem_in.at[i])
        for i, (src, dst) in enumerate((
            (later_hbm, later_v), (sel_hbm, sel), (rest_hbm, rest), (w_in_hbm, w_in),
            (bias_hbm, bias_v), (gain_hbm, gain_v), (shift_hbm, shift_v),
            (bias_mid_hbm, bias_mid_v), (live_hbm, live_v), (feat_hbm, feat),
            (trans_hbm, trans),
        ))
    ]
    for load in loads:
        load.start()
    w_copies = [
        pltpu.make_async_copy(
            w_mid_hbm.at[:, pl.ds(tap * CH, CH), :], w_mid.at[at % (AHEAD + 1)], sem_w.at[at]
        )
        for at, tap in enumerate(TAPS)
    ]
    for copy in w_copies[:AHEAD]:
        copy.start()

    groups = block_ones()
    for load in loads[:9]:
        load.wait()
    got = later_v[...].reshape(N_DEC * MSG_B, 128)
    w_cat = input_weights(w_in)
    bias = bias_v[...].reshape(1, CH)
    gain = gain_v[...].reshape(1, CH)
    shift = shift_v[...].reshape(1, CH)
    bias_mid = bias_mid_v[...].reshape(1, CH)
    flags = lax.dot_general(
        onehot(iota((8, 128), 1) == 0), got, (((1,), (1,)), ((), ())),
        preferred_element_type=F32,
    )
    flags = onehot(flags < 100.0)

    def entry_of(row):
        core, zz, xx, k = row // 256, (row // 64) % 4, (row // 16) % 4, (row // PART) % 2
        return (xx * 8 + zz * 2 + core) * CAP_C + k

    big = iota((512, 128), 0)
    held = dot(flags, onehot((big % PART == 0) & (entry_of(big) == iota((512, 128), 1))))
    before = onehot(iota((128, 128), 0) < iota((128, 128), 1))
    place = dot(held.astype(BF), before)
    take = onehot((held[:1] > 0.5) & (place[:1] == iota((32, 128), 0).astype(F32)))
    lane = iota((128, 512), 1)
    entry = entry_of(lane) == iota((128, 512), 0)
    take = dot(take, onehot(entry)).astype(BF)
    wide = jnp.concatenate([take] * 4, axis=0)
    kind = iota((128, 512), 0) // 32
    halves = [
        dot(jnp.where(iota((128, 512), 1) % PART == kind * 2 + half, wide, 0), got)
        for half in range(2)
    ]
    moved = jnp.concatenate(halves, axis=1)
    live_next = jnp.where(moved[:64, :1] < 32.0, 1.0, 0.0)
    fresh = jnp.where(moved > 32.0, 0.0, moved).astype(BF)
    pair = onehot(iota((64, 64), 1) == (iota((64, 64), 0) % 2) * 32 + iota((64, 64), 0) // 2)
    nlat_out[...] = dot(pair, fresh[64:]).astype(BF).reshape(32, 2, 256)
    outs = [pltpu.make_async_copy(nlat_out, nlat_hbm, sem_out.at[0])]
    outs[0].start()

    def put_mixed(cell, value):
        mixed[cell] = value

    features_of(patches(fresh, 64, sel, rest), 64, w_cat, bias, live_next, put_mixed,
                (REST_CELLS, PLAIN_CELLS))

    def put_next(cell, value):
        value = (value.astype(F32) * live_next).astype(BF)
        nact_out[:, :, cell * CH:(cell + 1) * CH] = dot(pair, value).astype(BF).reshape(32, 2, CH)

    normalised(lambda cell: mixed[cell], put_next, 64, groups, gain, shift)
    out = pltpu.make_async_copy(nact_out, nact_hbm, sem_out.at[1])
    out.start()
    outs.append(out)

    loads[9].wait()
    order = onehot(
        iota((128, 128), 1) == (iota((128, 128), 0) % 4) * 32 + iota((128, 128), 0) // 4
    )
    for cell in range(CELLS):
        turned = dot(order, feat[cell]).astype(BF).reshape(32, 4, CH)
        wide_out[:, :, cell * CH:(cell + 1) * CH] = turned
    feat_copy = pltpu.make_async_copy(wide_out, feat_out_hbm, sem_out.at[2])
    feat_copy.start()

    loads[10].wait()
    for at, tap in enumerate(TAPS):
        if at + AHEAD < len(TAPS):
            w_copies[at + AHEAD].start()
        w_copies[at].wait()
        here = at % (AHEAD + 1)
        g0 = w_mid[here, 0].astype(F32)
        g1 = w_mid[here, 1].astype(F32)
        g2 = w_mid[here, 2].astype(F32)
        ends = g0 + g2
        weights = [
            w_mid[here, 0], ((ends + g1) * 0.5).astype(BF), ((ends - g1) * 0.5).astype(BF),
            w_mid[here, 2],
        ]
        pairs = tap_cells(tap)
        for j in range(4):
            left = jnp.concatenate([trans[j, source] for _, source in pairs], axis=0)
            made = dot(left, weights[j])
            for i, (cell, _) in enumerate(pairs):
                piece = made[i * 64:(i + 1) * 64]
                if at == 0:
                    sums[j, cell] = piece
                else:
                    sums[j, cell] += piece

    r128 = iota((128, 128), 0)
    back = onehot(iota((128, 128), 1) == (r128 % 2) * 64 + ((r128 % 4) // 2) * 32 + r128 // 4)
    keep = live_v[...][:, :1]
    feat_copy.wait()
    for cell in range(CELLS):
        both = sums[1, cell] + sums[2, cell]
        apart = sums[1, cell] - sums[2, cell]
        even = ((sums[0, cell] + both + bias_mid) * keep).astype(BF)
        odd = ((apart - sums[3, cell] + bias_mid) * keep).astype(BF)
        turned = dot(back, jnp.concatenate([even, odd], axis=0)).astype(BF)
        wide_out[:, :, cell * CH:(cell + 1) * CH] = turned.reshape(32, 4, CH)
        if cell % 4 == 3:
            lanes = pl.ds((cell - 3) * CH, 4 * CH)
            out = pltpu.make_async_copy(
                wide_out.at[:, :, lanes], conv_hbm.at[:, :, lanes], sem_out.at[3 + cell // 4]
            )
            out.start()
            outs.append(out)
    for out in outs:
        out.wait()


def decode(trans, feat, live, later, weight_in, bias_in, gain, shift, bias_mid, sel, rest,
           weight_mid):
    hbm = pl.BlockSpec(memory_space=pltpu.HBM)
    wide = CELLS * CH
    dma = pltpu.SemaphoreType.DMA
    return pl.pallas_call(
        decode_kernel,
        out_shape=(
            jax.ShapeDtypeStruct((DSLOTS, FR, wide), BF),
            jax.ShapeDtypeStruct((DSLOTS, FR, wide), BF),
            jax.ShapeDtypeStruct((DSLOTS, 2, LAT * CELLS), BF),
            jax.ShapeDtypeStruct((DSLOTS, 2, wide), BF),
        ),
        in_specs=[hbm] * 12,
        out_specs=(hbm,) * 4,
        scratch_shapes=[
            pltpu.VMEM((4, CELLS, 64, CH), BF),
            pltpu.VMEM((CELLS, 128, CH), BF),
            pltpu.VMEM((64, 128), F32),
            pltpu.VMEM((2, 4, 4, MSG_B, 128), BF),
            pltpu.VMEM((3, 9 * LAT, CH), BF),
            pltpu.VMEM((CH,), F32),
            pltpu.VMEM((CH,), F32),
            pltpu.VMEM((CH,), F32),
            pltpu.VMEM((CH,), F32),
            pltpu.VMEM(sel.shape, BF),
            pltpu.VMEM(rest.shape, BF),
            pltpu.VMEM((AHEAD + 1, 3, CH, CH), BF),
            pltpu.VMEM((4, CELLS, 64, CH), F32),
            pltpu.VMEM((CELLS, 64, CH), BF),
            pltpu.VMEM((DSLOTS, FR, wide), BF),
            pltpu.VMEM((DSLOTS, 2, wide), BF),
            pltpu.VMEM((DSLOTS, 2, LAT * CELLS), BF),
            dma((11,)), dma((9,)), dma((7,)),
        ],
        compiler_params=pltpu.CompilerParams(vmem_limit_bytes=LIM),
        name="decode",
    )(trans, feat, live, later, weight_in, bias_in, gain, shift, bias_mid, sel, rest, weight_mid)


def shards(latent, latent_owner, next_owner, cache_latent, cache_act, weight_in, bias_in,
           norm_gain, norm_shift, weight_mid, bias_mid):
    sel, rest = patch_selectors()
    made = front(
        latent, latent_owner.reshape(1, GEN), next_owner.reshape(1, DSLOTS), cache_latent,
        cache_act, weight_in, bias_in, norm_gain, norm_shift, sel, rest,
    )
    return decode(*made, weight_in, bias_in, norm_gain, norm_shift, bias_mid, sel, rest, weight_mid)


def solution(mesh):
    both = ("gen", "dec")
    in_specs = (
        P(both, None, None), P(both, None), P(both), P(both, None, None), P(both, None, None),
        P(), P(), P(), P(), P(), P(),
    )
    out_specs = (P(both, None, None),) * 4
    return jax.shard_map(shards, mesh=mesh, in_specs=in_specs, out_specs=out_specs, check_vma=False)
```

time: 54 us -> 47.9 us (0.89)
  local copies, waits for them, and re-layouts: 3.43 us -> 0 us
  Pallas kernels: 49.6 us -> 47 us
    pallas_call x1, Pallas kernels: 30.9 us -> 24.8 us  [decode(): pl.pallas_call(decode_kernel, out_shape=(jax.ShapeDtypeStruct((DSLOTS, FR...]
    pallas_call x1, Pallas kernels: 18.7 us -> 22.2 us  [front(): pl.pallas_call(front_kernel, out_shape=(jax.ShapeDtypeStruct((4, CELLS, 6...]
    unnamed x10 -> x0, local copies, waits for them, and re-layouts: 3.43 us -> none
where the time goes in v1:
time: 47.9 us; the launch traced here: 47.8 us
  Pallas kernels  47 us (98%)
  between operations  0.8 us (2%)
    pallas_call x1, Pallas kernels, decode(): pl.pallas_call(decode_kernel, out_shape=(jax.ShapeDtypeStruct((DSLOTS, FR...  24.8 us
    pallas_call x1, Pallas kernels, front(): pl.pallas_call(front_kernel, out_shape=(jax.ShapeDtypeStruct((4, CELLS, 6...  22.2 us

profile of v1, /device:TPU:1, one launch (start us, length us, event | category | flops | bytes accessed | tf_op | source)
XLA Modules:
  0.0 47.8 jit_solution(13681966003239081928)
XLA Ops:
  0.6 22.2 %front.1 = (bf16[4,16,64,512]{3,2,1,0:T(8,128)(2,1)}, bf16[16,128,512]{2,1,0:T(8,128)(2,1)}, f32[64,128]{1,0:T(8,128)}, bf16[2,4,4,16,128]{4,3,2,1,0:T(8,128)(2,1)}) custom-call(bf16[24,4,256]{2,1,0:T(4,128)(2,1)} %latent_hbm.1, s32[1,24]{1,0:T(1,128)} %bitcast.2, s32[1,32]{1,0:T(1,128)} %bitcast.3, bf16[32,2,256]{2,1,0:T(2,128)(2,1)} %cache_hbm.1, ...), custom_call_target="tpu_custom_call" | custom-call | tf_op jit(solution)/shard_map/front/pallas_call | solution.py:352
  22.8 24.8 %decode.1 = (bf16[32,4,8192]{2,1,0:T(4,128)(2,1)}, bf16[32,4,8192]{2,1,0:T(4,128)(2,1)}, bf16[32,2,256]{2,1,0:T(2,128)(2,1)}, bf16[32,2,8192]{2,1,0:T(2,128)(2,1)}) custom-call(bf16[4,16,64,512]{3,2,1,0:T(8,128)(2,1)} %get-tuple-element.8.trans_hbm, bf16[16,128,512]{2,1,0:T(8,128)(2,1)} %get-tuple-element.9.feat_hbm, f32[64,128]{1,0:T(8,128)} %get-tuple-element.10.live_hbm, ...), custom_call_target="tpu_custom_call" | custom-call | tf_op jit(solution)/shard_map/decode/pallas_call | solution.py:540

commit v2 on v1

--- a/solution.py
+++ b/solution.py
@@ -158,21 +158,20 @@
     shift_hbm, sel_hbm, rest_hbm,
     trans_hbm, feat_hbm, live_hbm, later_hbm,
     latent, owner, nexts, cache, hist, w_in, bias_v, gain_v, shift_v, sel, rest,
-    send_a, recv_a, send_b, recv_x, recv_z, recv_c, feat, old, trans, live_v,
-    sem_in, sem_out, sem_sa, sem_ra, sem_sx, sem_rx, sem_sz, sem_rz, sem_sc, sem_rc,
+    send_a, recv_a, send_b, recv_x, recv_e, feat, old, trans, live_v,
+    sem_in, sem_out, sem_sa, sem_ra, sem_sx, sem_rx, sem_se, sem_re,
 ):
     g = lax.axis_index("gen")
     d = lax.axis_index("dec")
-    x, z, c = d // 8, (d // 2) % 4, d % 2
+    x, e = d // 8, d % 8
     gens = [lax.rem(g + i, 4) for i in (1, 2, 3)]
     xs = [lax.rem(x + i, 4) for i in (1, 2, 3)]
-    zs = [lax.rem(z + i, 4) for i in (1, 2, 3)]
+    es = [lax.rem(e + i, 8) for i in range(1, 8)]
     mesh_ids = pl.DeviceIdType.MESH
     barrier = pltpu.get_barrier_semaphore()
     peers = [{"gen": p} for p in gens]
-    peers += [{"dec": p * 8 + z * 2 + c} for p in xs]
-    peers += [{"dec": x * 8 + p * 2 + c} for p in zs]
-    peers += [{"dec": x * 8 + z * 2 + (1 - c)}]
+    peers += [{"dec": p * 8 + e} for p in xs]
+    peers += [{"dec": x * 8 + p} for p in es]
     for peer in peers:
         pl.semaphore_signal(barrier, inc=1, device_id=peer, device_id_type=mesh_ids)
 
@@ -249,21 +248,14 @@
         return pltpu.make_async_remote_copy(
             src_ref=send_b.at[target], dst_ref=recv_x.at[landed],
             send_sem=sem_sx.at[target], recv_sem=sem_rx.at[landed],
-            device_id={"dec": target * 8 + z * 2 + c}, device_id_type=mesh_ids,
+            device_id={"dec": target * 8 + e}, device_id_type=mesh_ids,
         )
 
-    def copy_z(target, landed):
+    def copy_e(target, landed):
         return pltpu.make_async_remote_copy(
-            src_ref=recv_x.at[:, target], dst_ref=recv_z.at[landed],
-            send_sem=sem_sz.at[target], recv_sem=sem_rz.at[landed],
-            device_id={"dec": x * 8 + target * 2 + c}, device_id_type=mesh_ids,
-        )
-
-    def copy_c(target, landed):
-        return pltpu.make_async_remote_copy(
-            src_ref=recv_z.at[:, :, target], dst_ref=recv_c.at[landed],
-            send_sem=sem_sc, recv_sem=sem_rc,
-            device_id={"dec": x * 8 + z * 2 + target}, device_id_type=mesh_ids,
+            src_ref=recv_x.at[:, target], dst_ref=recv_e.at[landed],
+            send_sem=sem_se.at[target], recv_sem=sem_re.at[landed],
+            device_id={"dec": x * 8 + target}, device_id_type=mesh_ids,
         )
 
     for p in xs:
@@ -286,9 +278,9 @@
 
     for p in xs:
         copy_x(p, p).wait_recv()
-    for p in zs:
-        copy_z(p, z).start()
-    recv_z[z] = recv_x[:, z]
+    for p in es:
+        copy_e(p, e).start()
+    recv_e[e] = recv_x[:, e]
 
     features_of(found, 128, w_cat, bias, live, put_feat, (PLAIN_CELLS,))
     outs = [pltpu.make_async_copy(feat, feat_hbm, sem_out.at[0]),
@@ -305,11 +297,6 @@
         off = feat[cell].astype(F32) - center
         square = square + off * off
     scale = lax.rsqrt(group_mean(square, groups) + EPSILON) * gain
-
-    for p in zs:
-        copy_z(p, p).wait_recv()
-    copy_c(1 - c, c).start()
-    recv_c[c] = recv_z[:, :, c]
 
     for cell in range(CELLS):
         u = (feat[cell].astype(F32) - center) * scale + shift
@@ -330,17 +317,17 @@
             out.start()
             outs.append(out)
 
-    copy_c(1 - c, 1 - c).wait_recv()
-    out = pltpu.make_async_copy(recv_c, later_hbm, sem_out.at[6])
+    for p in es:
+        copy_e(p, p).wait_recv()
+    out = pltpu.make_async_copy(recv_e, later_hbm, sem_out.at[6])
     out.start()
     outs.append(out)
     for p in gens:
         copy_a(p, g).wait_send()
     for p in xs:
         copy_x(p, x).wait_send()
-    for p in zs:
-        copy_z(p, z).wait_send()
-    copy_c(1 - c, c).wait_send()
+    for p in es:
+        copy_e(p, e).wait_send()
     for out in outs:
         out.wait()
 
@@ -355,7 +342,7 @@
             jax.ShapeDtypeStruct((4, CELLS, 64, CH), BF),
             jax.ShapeDtypeStruct((CELLS, 128, CH), BF),
             jax.ShapeDtypeStruct((64, 128), F32),
-            jax.ShapeDtypeStruct((2, 4, 4, MSG_B, 128), BF),
+            jax.ShapeDtypeStruct((8, 4, MSG_B, 128), BF),
         ),
         in_specs=[hbm] * 11,
         out_specs=(hbm,) * 4,
@@ -373,16 +360,14 @@
             pltpu.VMEM(rest.shape, BF),
             pltpu.VMEM((N_GEN, MSG_A, 128), BF),
             pltpu.VMEM((N_GEN, MSG_A, 128), BF),
-            pltpu.VMEM((4, 4, 2, MSG_B, 128), BF),
-            pltpu.VMEM((4, 4, 2, MSG_B, 128), BF),
-            pltpu.VMEM((4, 4, 2, MSG_B, 128), BF),
-            pltpu.VMEM((2, 4, 4, MSG_B, 128), BF),
+            pltpu.VMEM((4, 8, MSG_B, 128), BF),
+            pltpu.VMEM((4, 8, MSG_B, 128), BF),
+            pltpu.VMEM((8, 4, MSG_B, 128), BF),
             pltpu.VMEM((CELLS, 128, CH), BF),
             pltpu.VMEM((CELLS, 64, CH), BF),
             pltpu.VMEM((4, CELLS, 64, CH), BF),
             pltpu.VMEM((64, 128), F32),
-            dma((11,)), dma((7,)), dma((4,)), dma((4,)), dma((4,)), dma((4,)), dma((4,)), dma((4,)),
-            dma, dma,
+            dma((11,)), dma((7,)), dma((4,)), dma((4,)), dma((4,)), dma((4,)), dma((8,)), dma((8,)),
         ],
         compiler_params=pltpu.CompilerParams(
             collective_id=0, has_side_effects=True, vmem_limit_bytes=LIM
@@ -435,8 +420,7 @@
     flags = onehot(flags < 100.0)
 
     def entry_of(row):
-        core, zz, xx, k = row // 256, (row // 64) % 4, (row // 16) % 4, (row // PART) % 2
-        return (xx * 8 + zz * 2 + core) * CAP_C + k
+        return (((row // 16) % 4) * 8 + row // 64) * CAP_C + (row // PART) % CAP_C
 
     big = iota((512, 128), 0)
     held = dot(flags, onehot((big % PART == 0) & (entry_of(big) == iota((512, 128), 1))))
@@ -551,7 +535,7 @@
             pltpu.VMEM((4, CELLS, 64, CH), BF),
             pltpu.VMEM((CELLS, 128, CH), BF),
             pltpu.VMEM((64, 128), F32),
-            pltpu.VMEM((2, 4, 4, MSG_B, 128), BF),
+            pltpu.VMEM((8, 4, MSG_B, 128), BF),
             pltpu.VMEM((3, 9 * LAT, CH), BF),
             pltpu.VMEM((CH,), F32),
             pltpu.VMEM((CH,), F32),

time: 47.9 us -> 46.7 us (0.975)
  Pallas kernels: 47 us -> 45.6 us
    pallas_call x1, Pallas kernels: 22.2 us -> 20.8 us  [front(): pl.pallas_call(front_kernel, out_shape=(jax.ShapeDtypeStruct((4, CELLS, 6...]
where the time goes in v2:
time: 46.7 us; the launch traced here: 46.4 us
  Pallas kernels  45.6 us (98%)
  between operations  0.8 us (2%)
    pallas_call x1, Pallas kernels, decode(): pl.pallas_call(decode_kernel, out_shape=(jax.ShapeDtypeStruct((DSLOTS, FR...  24.7 us
    pallas_call x1, Pallas kernels, front(): pl.pallas_call(front_kernel, out_shape=(jax.ShapeDtypeStruct((4, CELLS, 6...  20.8 us

profile of v2, /device:TPU:1, one launch (start us, length us, event | category | flops | bytes accessed | tf_op | source)
XLA Modules:
  0.0 46.4 jit_solution(10241823144879462424)
XLA Ops:
  0.6 20.8 %front.1 = (bf16[4,16,64,512]{3,2,1,0:T(8,128)(2,1)}, bf16[16,128,512]{2,1,0:T(8,128)(2,1)}, f32[64,128]{1,0:T(8,128)}, bf16[8,4,16,128]{3,2,1,0:T(8,128)(2,1)}) custom-call(bf16[24,4,256]{2,1,0:T(4,128)(2,1)} %latent_hbm.1, s32[1,24]{1,0:T(1,128)} %bitcast.2, s32[1,32]{1,0:T(1,128)} %bitcast.3, bf16[32,2,256]{2,1,0:T(2,128)(2,1)} %cache_hbm.1, ...), custom_call_target="tpu_custom_call" | custom-call | tf_op jit(solution)/shard_map/front/pallas_call | solution.py:339
  21.5 24.7 %decode.1 = (bf16[32,4,8192]{2,1,0:T(4,128)(2,1)}, bf16[32,4,8192]{2,1,0:T(4,128)(2,1)}, bf16[32,2,256]{2,1,0:T(2,128)(2,1)}, bf16[32,2,8192]{2,1,0:T(2,128)(2,1)}) custom-call(bf16[4,16,64,512]{3,2,1,0:T(8,128)(2,1)} %get-tuple-element.8.trans_hbm, bf16[16,128,512]{2,1,0:T(8,128)(2,1)} %get-tuple-element.9.feat_hbm, f32[64,128]{1,0:T(8,128)} %get-tuple-element.10.live_hbm, ...), custom_call_target="tpu_custom_call" | custom-call | tf_op jit(solution)/shard_map/decode/pallas_call | solution.py:524

commit v3 on v2

--- a/solution.py
+++ b/solution.py
@@ -158,7 +158,7 @@
     shift_hbm, sel_hbm, rest_hbm,
     trans_hbm, feat_hbm, live_hbm, later_hbm,
     latent, owner, nexts, cache, hist, w_in, bias_v, gain_v, shift_v, sel, rest,
-    send_a, recv_a, send_b, recv_x, recv_e, feat, old, trans, live_v,
+    send_a, recv_a, send_b, recv_x, recv_e, feat, trans, live_v,
     sem_in, sem_out, sem_sa, sem_ra, sem_sx, sem_rx, sem_se, sem_re,
 ):
     g = lax.axis_index("gen")
@@ -184,6 +184,9 @@
         load = pltpu.make_async_copy(src, dst, sem_in.at[i])
         load.start()
         loads.append(load)
+
+    groups = block_ones()
+    turn = onehot(iota((64, 64), 1) == (iota((64, 64), 0) % 32) * 2 + iota((64, 64), 0) // 32)
 
     loads[0].wait()
     loads[1].wait()
@@ -224,14 +227,9 @@
     filled = jnp.sum(jnp.where(pick_b, 1.0, 0.0), axis=1, keepdims=True)
     pick_b = onehot(pick_b)
     loads[4].wait()
-    turn = onehot(iota((64, 64), 1) == (iota((64, 64), 0) % 32) * 2 + iota((64, 64), 0) // 32)
-    for cell in range(CELLS):
-        lanes_c = slice(cell * CH, (cell + 1) * CH)
-        old[cell] = dot(turn, hist[:, :, lanes_c].reshape(64, CH)).astype(BF)
     loads[3].wait()
     for load in loads[5:]:
         load.wait()
-    groups = block_ones()
     w_cat = input_weights(w_in)
     bias = bias_v[...].reshape(1, CH)
     gain = gain_v[...].reshape(1, CH)
@@ -276,13 +274,13 @@
 
     features_of(found, 128, w_cat, bias, live, put_feat, (REST_CELLS,))
 
+    features_of(found, 128, w_cat, bias, live, put_feat, (PLAIN_CELLS,))
+
     for p in xs:
         copy_x(p, p).wait_recv()
     for p in es:
         copy_e(p, e).start()
     recv_e[e] = recv_x[:, e]
-
-    features_of(found, 128, w_cat, bias, live, put_feat, (PLAIN_CELLS,))
     outs = [pltpu.make_async_copy(feat, feat_hbm, sem_out.at[0]),
             pltpu.make_async_copy(live_v, live_hbm, sem_out.at[1])]
     for out in outs:
@@ -301,7 +299,8 @@
     for cell in range(CELLS):
         u = (feat[cell].astype(F32) - center) * scale + shift
         act = silu(u).astype(BF)
-        q = [old[cell, :32], old[cell, 32:]] + [act[t * 32:t * 32 + 32] for t in range(4)]
+        old = dot(turn, hist[:, :, cell * CH:(cell + 1) * CH].reshape(64, CH)).astype(BF)
+        q = [old[:32], old[32:]] + [act[t * 32:t * 32 + 32] for t in range(4)]
         for tile in range(2):
             d0, d1, d2, d3 = q[2 * tile:2 * tile + 4]
             at = slice(tile * 32, tile * 32 + 32)
@@ -309,17 +308,17 @@
             trans[1, cell, at] = d1 + d2
             trans[2, cell, at] = d2 - d1
             trans[3, cell, at] = d1 - d3
-        if cell % 4 == 3:
-            part = pl.ds(cell - 3, 4)
+        if cell % 2 == 1:
+            part = pl.ds(cell - 1, 2)
             out = pltpu.make_async_copy(
-                trans.at[:, part], trans_hbm.at[:, part], sem_out.at[2 + cell // 4]
+                trans.at[:, part], trans_hbm.at[:, part], sem_out.at[2 + cell // 2]
             )
             out.start()
             outs.append(out)
 
     for p in es:
         copy_e(p, p).wait_recv()
-    out = pltpu.make_async_copy(recv_e, later_hbm, sem_out.at[6])
+    out = pltpu.make_async_copy(recv_e, later_hbm, sem_out.at[10])
     out.start()
     outs.append(out)
     for p in gens:
@@ -364,10 +363,9 @@
             pltpu.VMEM((4, 8, MSG_B, 128), BF),
             pltpu.VMEM((8, 4, MSG_B, 128), BF),
             pltpu.VMEM((CELLS, 128, CH), BF),
-            pltpu.VMEM((CELLS, 64, CH), BF),
             pltpu.VMEM((4, CELLS, 64, CH), BF),
             pltpu.VMEM((64, 128), F32),
-            dma((11,)), dma((7,)), dma((4,)), dma((4,)), dma((4,)), dma((4,)), dma((8,)), dma((8,)),
+            dma((11,)), dma((11,)), dma((4,)), dma((4,)), dma((4,)), dma((4,)), dma((8,)), dma((8,)),
         ],
         compiler_params=pltpu.CompilerParams(
             collective_id=0, has_side_effects=True, vmem_limit_bytes=LIM
@@ -405,14 +403,8 @@
         copy.start()
 
     groups = block_ones()
-    for load in loads[:9]:
-        load.wait()
+    loads[0].wait()
     got = later_v[...].reshape(N_DEC * MSG_B, 128)
-    w_cat = input_weights(w_in)
-    bias = bias_v[...].reshape(1, CH)
-    gain = gain_v[...].reshape(1, CH)
-    shift = shift_v[...].reshape(1, CH)
-    bias_mid = bias_mid_v[...].reshape(1, CH)
     flags = lax.dot_general(
         onehot(iota((8, 128), 1) == 0), got, (((1,), (1,)), ((), ())),
         preferred_element_type=F32,
@@ -444,28 +436,36 @@
     outs = [pltpu.make_async_copy(nlat_out, nlat_hbm, sem_out.at[0])]
     outs[0].start()
 
+    for load in loads[1:9]:
+        load.wait()
+    w_cat = input_weights(w_in)
+    bias = bias_v[...].reshape(1, CH)
+    gain = gain_v[...].reshape(1, CH)
+    shift = shift_v[...].reshape(1, CH)
+    bias_mid = bias_mid_v[...].reshape(1, CH)
+
     def put_mixed(cell, value):
         mixed[cell] = value
 
     features_of(patches(fresh, 64, sel, rest), 64, w_cat, bias, live_next, put_mixed,
                 (REST_CELLS, PLAIN_CELLS))
 
+    order = onehot(
+        iota((128, 128), 1) == (iota((128, 128), 0) % 4) * 32 + iota((128, 128), 0) // 4
+    )
+
     def put_next(cell, value):
+        turned = dot(order, feat[cell]).astype(BF).reshape(32, 4, CH)
+        wide_out[:, :, cell * CH:(cell + 1) * CH] = turned
         value = (value.astype(F32) * live_next).astype(BF)
         nact_out[:, :, cell * CH:(cell + 1) * CH] = dot(pair, value).astype(BF).reshape(32, 2, CH)
 
+    loads[9].wait()
     normalised(lambda cell: mixed[cell], put_next, 64, groups, gain, shift)
     out = pltpu.make_async_copy(nact_out, nact_hbm, sem_out.at[1])
     out.start()
     outs.append(out)
 
-    loads[9].wait()
-    order = onehot(
-        iota((128, 128), 1) == (iota((128, 128), 0) % 4) * 32 + iota((128, 128), 0) // 4
-    )
-    for cell in range(CELLS):
-        turned = dot(order, feat[cell]).astype(BF).reshape(32, 4, CH)
-        wide_out[:, :, cell * CH:(cell + 1) * CH] = turned
     feat_copy = pltpu.make_async_copy(wide_out, feat_out_hbm, sem_out.at[2])
     feat_copy.start()
 
@@ -505,10 +505,10 @@
         odd = ((apart - sums[3, cell] + bias_mid) * keep).astype(BF)
         turned = dot(back, jnp.concatenate([even, odd], axis=0)).astype(BF)
         wide_out[:, :, cell * CH:(cell + 1) * CH] = turned.reshape(32, 4, CH)
-        if cell % 4 == 3:
-            lanes = pl.ds((cell - 3) * CH, 4 * CH)
+        if cell % 2 == 1:
+            lanes = pl.ds((cell - 1) * CH, 2 * CH)
             out = pltpu.make_async_copy(
-                wide_out.at[:, :, lanes], conv_hbm.at[:, :, lanes], sem_out.at[3 + cell // 4]
+                wide_out.at[:, :, lanes], conv_hbm.at[:, :, lanes], sem_out.at[3 + cell // 2]
             )
             out.start()
             outs.append(out)
@@ -549,7 +549,7 @@
             pltpu.VMEM((DSLOTS, FR, wide), BF),
             pltpu.VMEM((DSLOTS, 2, wide), BF),
             pltpu.VMEM((DSLOTS, 2, LAT * CELLS), BF),
-            dma((11,)), dma((9,)), dma((7,)),
+            dma((11,)), dma((9,)), dma((11,)),
         ],
         compiler_params=pltpu.CompilerParams(vmem_limit_bytes=LIM),
         name="decode",

time: 46.7 us -> 45.4 us (0.972)
  Pallas kernels: 45.6 us -> 44.5 us
    pallas_call x1, Pallas kernels: 24.7 us -> 23.8 us  [decode(): pl.pallas_call(decode_kernel, out_shape=(jax.ShapeDtypeStruct((DSLOTS, FR...]
where the time goes in v3:
time: 45.4 us; the launch traced here: 45.3 us
  Pallas kernels  44.5 us (98%)
  between operations  0.8 us (2%)
    pallas_call x1, Pallas kernels, decode(): pl.pallas_call(decode_kernel, out_shape=(jax.ShapeDtypeStruct((DSLOTS, FR...  23.8 us
    pallas_call x1, Pallas kernels, front(): pl.pallas_call(front_kernel, out_shape=(jax.ShapeDtypeStruct((4, CELLS, 6...  20.7 us

profile of v3, /device:TPU:1, one launch (start us, length us, event | category | flops | bytes accessed | tf_op | source)
XLA Modules:
  0.0 45.3 jit_solution(15460863420029163337)
XLA Ops:
  0.6 20.7 %front.1 = (bf16[4,16,64,512]{3,2,1,0:T(8,128)(2,1)}, bf16[16,128,512]{2,1,0:T(8,128)(2,1)}, f32[64,128]{1,0:T(8,128)}, bf16[8,4,16,128]{3,2,1,0:T(8,128)(2,1)}) custom-call(bf16[24,4,256]{2,1,0:T(4,128)(2,1)} %latent_hbm.1, s32[1,24]{1,0:T(1,128)} %bitcast.2, s32[1,32]{1,0:T(1,128)} %bitcast.3, bf16[32,2,256]{2,1,0:T(2,128)(2,1)} %cache_hbm.1, ...), custom_call_target="tpu_custom_call" | custom-call | tf_op jit(solution)/shard_map/front/pallas_call | solution.py:338
  21.3 23.8 %decode.1 = (bf16[32,4,8192]{2,1,0:T(4,128)(2,1)}, bf16[32,4,8192]{2,1,0:T(4,128)(2,1)}, bf16[32,2,256]{2,1,0:T(2,128)(2,1)}, bf16[32,2,8192]{2,1,0:T(2,128)(2,1)}) custom-call(bf16[4,16,64,512]{3,2,1,0:T(8,128)(2,1)} %get-tuple-element.8.trans_hbm, bf16[16,128,512]{2,1,0:T(8,128)(2,1)} %get-tuple-element.9.feat_hbm, f32[64,128]{1,0:T(8,128)} %get-tuple-element.10.live_hbm, ...), custom_call_target="tpu_custom_call" | custom-call | tf_op jit(solution)/shard_map/decode/pallas_call | solution.py:524

commit v4 on v3

--- a/solution.py
+++ b/solution.py
@@ -269,8 +269,11 @@
     fresh = jnp.where(placed > 32.0, 0.0, placed).astype(BF)
     found = patches(jnp.concatenate([cached, fresh], axis=0), 128, sel, rest)
 
+    total = [jnp.zeros((128, CH), F32)]
+
     def put_feat(cell, value):
         feat[cell] = value
+        total[0] = total[0] + value.astype(F32)
 
     features_of(found, 128, w_cat, bias, live, put_feat, (REST_CELLS,))
 
@@ -286,10 +289,7 @@
     for out in outs:
         out.start()
 
-    total = jnp.zeros((128, CH), F32)
-    for cell in range(CELLS):
-        total = total + feat[cell].astype(F32)
-    center = group_mean(total, groups)
+    center = group_mean(total[0], groups)
     square = jnp.zeros((128, CH), F32)
     for cell in range(CELLS):
         off = feat[cell].astype(F32) - center

time: 45.4 us -> 45.7 us (level)
  no operation moved by 1% of the time
where the time goes in v4:
time: 45.7 us; the launch traced here: 45.5 us
  Pallas kernels  44.7 us (98%)
  between operations  0.8 us (2%)
    pallas_call x1, Pallas kernels, decode(): pl.pallas_call(decode_kernel, out_shape=(jax.ShapeDtypeStruct((DSLOTS, FR...  23.8 us
    pallas_call x1, Pallas kernels, front(): pl.pallas_call(front_kernel, out_shape=(jax.ShapeDtypeStruct((4, CELLS, 6...  20.9 us

profile of v4, /device:TPU:1, one launch (start us, length us, event | category | flops | bytes accessed | tf_op | source)
XLA Modules:
  0.0 45.5 jit_solution(11667805896563997414)
XLA Ops:
  0.6 20.9 %front.1 = (bf16[4,16,64,512]{3,2,1,0:T(8,128)(2,1)}, bf16[16,128,512]{2,1,0:T(8,128)(2,1)}, f32[64,128]{1,0:T(8,128)}, bf16[8,4,16,128]{3,2,1,0:T(8,128)(2,1)}) custom-call(bf16[24,4,256]{2,1,0:T(4,128)(2,1)} %latent_hbm.1, s32[1,24]{1,0:T(1,128)} %bitcast.2, s32[1,32]{1,0:T(1,128)} %bitcast.3, bf16[32,2,256]{2,1,0:T(2,128)(2,1)} %cache_hbm.1, ...), custom_call_target="tpu_custom_call" | custom-call | tf_op jit(solution)/shard_map/front/pallas_call | solution.py:338
  21.6 23.8 %decode.1 = (bf16[32,4,8192]{2,1,0:T(4,128)(2,1)}, bf16[32,4,8192]{2,1,0:T(4,128)(2,1)}, bf16[32,2,256]{2,1,0:T(2,128)(2,1)}, bf16[32,2,8192]{2,1,0:T(2,128)(2,1)}) custom-call(bf16[4,16,64,512]{3,2,1,0:T(8,128)(2,1)} %get-tuple-element.8.trans_hbm, bf16[16,128,512]{2,1,0:T(8,128)(2,1)} %get-tuple-element.9.feat_hbm, f32[64,128]{1,0:T(8,128)} %get-tuple-element.10.live_hbm, ...), custom_call_target="tpu_custom_call" | custom-call | tf_op jit(solution)/shard_map/decode/pallas_call | solution.py:524
